TPU v7x, 128 devices: a whole 4x4x4 slice. The times are simulated.
128 devices in a mesh: seq: 4 (over x), shard: 32 (over z, y, core).
Axes of the slice: x: 4, y: 4, z: 4, core: 2. Of those that a mesh axis runs over, the one named last changes fastest.
Arguments:
- inputs: bfloat16 [32, 2048, 768], P('shard', 'seq'), may hold values from -6 to 6
- positions: int32 [32, 2048], P('shard', 'seq'), may hold values from 0 to 2045, as said below
- first_gain: bfloat16 [768], P('shard'), may hold values from 0.5 to 1.5
- first_shift: bfloat16 [768], P('shard'), may hold values from -1 to 1
- second_gain: bfloat16 [768], P('shard'), may hold values from 0.5 to 1.5
- second_shift: bfloat16 [768], P('shard'), may hold values from -1 to 1
- mix_weight: bfloat16 [768, 2304], P('shard'), may hold values from -0.21875 to 0.21875
- mix_bias: bfloat16 [2304], P('shard'), may hold values from -1 to 1
- out_weight: bfloat16 [768, 768], P('shard'), may hold values from -0.875 to 0.875
- out_bias: bfloat16 [768], P('shard'), may hold values from -1 to 1
- up_weight: bfloat16 [768, 3072], P('shard'), may hold values from -0.21875 to 0.21875
- up_bias: bfloat16 [3072], P('shard'), may hold values from -1 to 1
- down_weight: bfloat16 [3072, 768], P('shard'), may hold values from -0.109375 to 0.109375
- down_bias: bfloat16 [768], P('shard'), may hold values from -1 to 1
- cotangent: bfloat16 [32, 2048, 768], P('shard', 'seq'), may hold values from -6 to 6
Outputs:
- outputs: bfloat16 [32, 2048, 768], P('shard', 'seq')
- input_grad: bfloat16 [32, 2048, 768], P('shard', 'seq')
- grad_first_gain: float32 [768], P('shard')
- grad_first_shift: float32 [768], P('shard')
- grad_second_gain: float32 [768], P('shard')
- grad_second_shift: float32 [768], P('shard')
- grad_mix_weight: float32 [768, 2304], P('shard')
- grad_mix_bias: float32 [2304], P('shard')
- grad_out_weight: float32 [768, 768], P('shard')
- grad_out_bias: float32 [768], P('shard')
- grad_up_weight: float32 [768, 3072], P('shard')
- grad_up_bias: float32 [3072], P('shard')
- grad_down_weight: float32 [3072, 768], P('shard')
- grad_down_bias: float32 [768], P('shard')
Inputs may be any that keep to these rules, and one draw needn't show every extreme that they name: Each sequence is three documents laid end to end, positions counting 0, 1, 2, ... from each document's start; the middle document starts within the first 512 tokens, after the first token, and ends within the last 512, before the last token. In one sequence, drawn from the seed, the middle document runs from token 1 to token 2046.
All inputs are finite; a program needn't handle non-finite values.
Results may differ from a plain program's by a relative error of at most 0.02.
Values may be sent and summed in bfloat16 or wider, within the bound.
A program may use at most 192 MiB of HBM per device.

v0:
```python
import functools

import jax
import jax.numpy as jnp
from jax import lax
from jax.experimental import pallas as pl
from jax.experimental.pallas import tpu as pltpu
from jax.sharding import PartitionSpec as P

HD = 64
ROT = 16
NX = 4
BF = jnp.bfloat16
F32 = jnp.float32
MESH = pl.DeviceIdType.MESH
NT = (((1,), (1,)), ((), ()))
VMEM_LIMIT = 56 * 1024 * 1024
WIDE = 1536
PAIR = 48


def dot(a, b):
    return jnp.dot(a, b, preferred_element_type=F32)


def dot_nt(a, b):
    return lax.dot_general(a, b, NT, preferred_element_type=F32)


def dot_tn(a, b):
    return lax.dot_general(a, b, (((0,), (0,)), ((), ())), preferred_element_type=F32)


def places():
    x = lax.axis_index("seq")
    s = lax.axis_index("shard")
    return x, s // 8, (s // 2) % 4, s % 2


def at(x, z, y, c):
    return (x, (z * 4 + y) * 2 + c)


ERFC = (0.254829592, -0.284496736, 1.421413741, -1.453152027, 1.061405429)


def gelu_and_slope(h):
    t = 1.0 / (1.0 + (0.3275911 * 2.0**-0.5) * jnp.abs(h))
    e = jnp.exp(h * h * -0.5)
    poly = t * (ERFC[0] + t * (ERFC[1] + t * (ERFC[2] + t * (ERFC[3] + t * ERFC[4]))))
    tail_part = 0.5 * poly * e
    cdf = jnp.where(h >= 0, 1.0 - tail_part, tail_part)
    return h * cdf, cdf + h * e * 0.3989422804014327


def iota(shape, dim):
    return lax.broadcasted_iota(jnp.int32, shape, dim)


def front_kernel(
    rows_ref, grad_ref, pair_ref, pos_ref,
    mixed_o, act_o, actt_o, slope_o, unitt_o, cg_o, w_o, vec_o, table_o,
    rows_all, w, pos_all, grad, mixed, act, actt, slope, unitt, cg, cgs, vec, table,
    s1, r1, s2, r2, s3, r3, sx, rx, sf, rf, sp, rp, sc, rc, loc, wr,
):
    x, z, y, c = places()
    is0 = c == 0
    right, left, far = lax.rem(x + 1, 4), lax.rem(x + 3, 4), lax.rem(x + 2, 4)
    me = lax.axis_index("shard")
    mine, other = w.at[c], w.at[1 - c]

    def first(k):
        return at(x, jnp.where(is0, z, lax.rem(z + k, 4)), jnp.where(is0, lax.rem(y + k, 4), y), c)

    def second(k):
        return at(x, jnp.where(is0, lax.rem(z + k, 4), z), jnp.where(is0, y, lax.rem(y + k, 4)), c)

    def block(dz, dy):
        return lax.rem(z + dz, 4) * 4 + lax.rem(y + dy, 4)

    def held(a, b):
        da, db = (4 - a) % 4, (4 - b) % 4
        return jnp.where(is0, block(db, da), block(da, db))

    def rows_of(ref, b):
        return ref.at[pl.ds(pl.multiple_of(b * PAIR, 16), PAIR)]

    def quarter(who, q):
        return rows_all.at[pl.ds(pl.multiple_of(who * 512 + q * 128, 128), 128)]

    def remote(src, dst, ss, rs, dev):
        return pltpu.make_async_remote_copy(
            src_ref=src, dst_ref=dst, send_sem=ss, recv_sem=rs, device_id=dev, device_id_type=MESH
        )

    started = []

    def send(*args):
        cp = remote(*args)
        cp.start()
        started.append(cp)

    sibling = (x, me + 1 - 2 * c)

    def landed(dst, sem):
        remote(dst, dst, sem, sem, sibling).wait_recv()

    own_block = z * 4 + y
    own_pos = pos_all.at[pl.ds(pl.multiple_of(x * 8, 8), 8)]
    local_copies = []
    for n, (src, dst) in enumerate(
        (
            (pair_ref, rows_of(mine, own_block)),
            (rows_ref, rows_all.at[pl.ds(pl.multiple_of(x * 512, 512), 512)]),
            (pos_ref, own_pos),
            (grad_ref, grad),
        )
    ):
        cp = pltpu.make_async_copy(src, dst, loc.at[n])
        cp.start()
        local_copies.append(cp)
    barrier = pltpu.get_barrier_semaphore()
    peers = [first(k) for k in (1, 2, 3)] + [second(k) for k in (1, 2, 3)]
    peers += [sibling, (right, me), (left, me), (far, me)]
    for peer in peers:
        pl.semaphore_signal(barrier, inc=1, device_id=peer, device_id_type=MESH)
    pl.semaphore_wait(barrier, len(peers))

    order = (1, 3, 2)
    for k in order:
        send(pair_ref, rows_of(mine, own_block), s1.at[k - 1], r1.at[k - 1], first(k))
    own = [rows_ref.at[pl.ds(q * 128, 128)] for q in range(4)]
    for i in range(4):
        send(own[i], quarter(x, i), sx.at[0, i], rx.at[0, i], (right, me))
        send(own[3 - i], quarter(x, 3 - i), sx.at[1, 3 - i], rx.at[1, 3 - i], (left, me))
    for k in order:
        send(pair_ref, rows_of(mine, own_block), s2.at[0, k - 1], r2.at[0, k - 1], second(k))
    send(pair_ref, rows_of(mine, own_block), s3.at[0, 0], r3.at[0, 0], sibling)
    for k in order:
        send(pos_ref, own_pos, sp.at[k - 1], rp.at[k - 1], (lax.rem(x + k, 4), me))
    for cp in local_copies:
        cp.wait()

    for k in order:
        b = held(k, 0)
        landed(rows_of(mine, b), r1.at[k - 1])
        for j in order:
            send(rows_of(mine, b), rows_of(mine, b), s2.at[k, j - 1], r2.at[k, j - 1], second(j))
        send(rows_of(mine, b), rows_of(mine, b), s3.at[k, 0], r3.at[k, 0], sibling)

    for k in order:
        src = lax.rem(x + 4 - k, 4)
        landed(pos_all.at[pl.ds(pl.multiple_of(src * 8, 8), 8)], rp.at[k - 1])
    place = jnp.concatenate(
        [pos_all[8 * d + q : 8 * d + q + 1] for d in range(4) for q in range(4)], axis=1
    ).astype(F32)
    freqs = jnp.ones((8, 2048), F32)
    for n in range(1, 8):
        freqs = jnp.where(iota((8, 2048), 0) == n, 10000.0 ** (-2.0 * n / ROT), freqs)
    angles = place * freqs
    cos8, sin8 = jnp.cos(angles), jnp.sin(angles)
    start = jnp.broadcast_to(iota((1, 2048), 1).astype(F32) - place, (8, 2048))
    table[...] = jnp.concatenate(
        [cos8, cos8, jnp.ones((48, 2048), F32), sin8, sin8, start, jnp.zeros((40, 2048), F32)], axis=0
    ).T

    for i in range(2):
        landed(quarter(left, i), rx.at[0, i])
        send(quarter(left, i), quarter(left, i), sf.at[0, i], rf.at[0, i], (right, me))
        landed(quarter(right, 3 - i), rx.at[1, 3 - i])
        send(quarter(right, 3 - i), quarter(right, 3 - i), sf.at[1, i], rf.at[1, i], (left, me))
    for j in order:
        for k in (0,) + order:
            b = held(k, j)
            landed(rows_of(mine, b), r2.at[k, j - 1])
            send(rows_of(mine, b), rows_of(mine, b), s3.at[k, j], r3.at[k, j], sibling)
    for a in range(4):
        for b in range(4):
            da, db = (4 - a) % 4, (4 - b) % 4
            blk = jnp.where(is0, block(da, db), block(db, da))
            landed(rows_of(other, blk), r3.at[a, b])

    own_tok = pl.ds(pl.multiple_of(x * 512, 512), 512)
    for k in (2, 1, 3, 0):
        dev = lax.rem(x + k, 4)
        heads = w[0, pl.ds(pl.multiple_of(dev * 192, 64), 192), 0:768]

        @pl.loop(0, 2)
        def _(i):
            r = pl.ds(pl.multiple_of(i * 256, 256), 256)
            cgs[k, r] = dot_nt(grad[r], heads).astype(BF)

        if k:
            send(cgs.at[k], cg.at[own_tok], sc.at[k - 1], rc.at[k - 1], (dev, me))
        else:
            cg[own_tok] = cgs[0]

    packed = w[0, :, 1344:1536]
    pick = [dot((iota((32, 768), 1) == 24 * iota((32, 768), 0) + n).astype(BF), packed).astype(BF) for n in range(2)]

    def spread(src, width, base, group, shift):
        lane = iota((192, width), 1)
        one_hot = iota((192, width), 0) == lax.rem(lane, group) + base
        lane = iota((32, width), 1)
        keep = iota((32, width), 0) == lax.div(lane, group) + shift
        return jnp.sum(jnp.where(keep, dot(src, one_hot.astype(BF)), 0.0), axis=0, keepdims=True)

    g1, b1, g2, b2, out_b, down_b = (spread(pick[0], 768, 24 * n, 24, 0) for n in range(6))
    mix_b = spread(pick[1], 576, 0, 72, 8 * x)
    up_b = spread(pick[1], 768, 72 + 24 * x, 24, 0)
    vec[...] = jnp.concatenate([g1, b1, g2, b2, out_b + down_b, up_b, g1, g1], axis=0)

    writes = []

    def write(src, dst):
        cp = pltpu.make_async_copy(src, dst, wr.at[len(writes)])
        cp.start()
        writes.append(cp)

    write(w, w_o)
    write(vec, vec_o)
    write(table, table_o)

    def compute(who):
        @pl.loop(0, 2)
        def _(i):
            r = pl.ds(pl.multiple_of(who * 512 + i * 256, 256), 256)
            v = rows_all[r].astype(F32)
            v = v - jnp.mean(v, axis=-1, keepdims=True)
            unit = v * lax.rsqrt(jnp.mean(v * v, axis=-1, keepdims=True) + 1e-05)
            cols = pl.ds(pl.multiple_of(i * 256, 256), 256)
            unitt[who, :, cols] = unit.astype(BF).T
            one = (unit * vec[0:1] + vec[1:2]).astype(BF)
            mixed[r] = (dot(one, w[0, :, 768:1344]) + mix_b).astype(BF)
            two = (unit * vec[2:3] + vec[3:4]).astype(BF)
            hidden = dot(two, w[1, :, 0:768]) + vec[5:6]
            a, s = gelu_and_slope(hidden)
            a = a.astype(BF)
            act[r] = a
            actt[who, :, cols] = a.T
            slope[r] = s.astype(BF)

        t = pl.ds(pl.multiple_of(who * 512, 512), 512)
        write(mixed.at[t], mixed_o.at[t])
        write(act.at[t], act_o.at[t])
        write(slope.at[t], slope_o.at[t])
        write(actt.at[who], actt_o.at[who])
        write(unitt.at[who], unitt_o.at[who])

    compute(x)
    for i in range(2):
        landed(quarter(left, 2 + i), rx.at[0, 2 + i])
    compute(left)
    for i in range(2):
        landed(quarter(right, i), rx.at[1, i])
    compute(right)
    for i in range(2):
        landed(quarter(far, i), rf.at[0, i])
        landed(quarter(far, 3 - i), rf.at[1, i])
    compute(far)
    for k in (1, 3, 2):
        t = pl.ds(pl.multiple_of(lax.rem(x + 4 - k, 4) * 512, 512), 512)
        landed(cg.at[t], rc.at[k - 1])
    write(cg, cg_o)
    for cp in writes:
        cp.wait()
    for cp in started:
        cp.wait_send()


def front(rows, grad, pair, pos):
    hbm = pl.BlockSpec(memory_space=pl.ANY)
    dma = pltpu.SemaphoreType.DMA
    outs = [
        ((2048, 576), BF), ((2048, 768), BF), ((4, 768, 512), BF), ((2048, 768), BF), ((4, 768, 512), BF),
        ((2048, 192), BF), ((2, 768, WIDE), BF), ((8, 768), F32), ((2048, 128), F32),
    ]
    return pl.pallas_call(
        front_kernel,
        out_shape=tuple(jax.ShapeDtypeStruct(s, t) for s, t in outs),
        in_specs=[hbm] * 4,
        out_specs=[hbm] * 9,
        scratch_shapes=[
            pltpu.VMEM((2048, 768), BF),
            pltpu.VMEM((2, 768, WIDE), BF),
            pltpu.VMEM((32, 128), jnp.int32),
            pltpu.VMEM((512, 768), BF),
            pltpu.VMEM((2048, 576), BF),
            pltpu.VMEM((2048, 768), BF),
            pltpu.VMEM((4, 768, 512), BF),
            pltpu.VMEM((2048, 768), BF),
            pltpu.VMEM((4, 768, 512), BF),
            pltpu.VMEM((2048, 192), BF),
            pltpu.VMEM((4, 512, 192), BF),
            pltpu.VMEM((8, 768), F32),
            pltpu.VMEM((2048, 128), F32),
            dma((3,)), dma((3,)), dma((4, 3)), dma((4, 3)), dma((4, 4)), dma((4, 4)),
            dma((2, 4)), dma((2, 4)), dma((2, 2)), dma((2, 2)), dma((3,)), dma((3,)), dma((3,)), dma((3,)),
            dma((4,)), dma((24,)),
        ],
        compiler_params=pltpu.CompilerParams(
            collective_id=0, has_side_effects=True, vmem_limit_bytes=VMEM_LIMIT
        ),
        name="front_all",
    )(rows, grad, pair, pos)


BQ = 512
NB = 2048 // BQ


def attention_kernel(
    mixed_ref, table_ref, grad_ref, ctx_ref, ctxt_ref, out_ref,
    qs, ks, vs, qt, es, ss, dkt, dvt, dqs, os, gs,
):
    row, lane = iota((64, 64), 0), iota((64, 64), 1)
    turn = jnp.where((lane == row + 8) & (row < 8), 1.0, jnp.where((row == lane + 8) & (lane < 8), -1.0, 0.0))
    turn = turn.astype(BF)

    def angles(r):
        t = table_ref[r]
        return t[:, 0:64], jnp.where(iota((BQ, 64), 1) < ROT, t[:, 64:128], 0.0)

    @pl.loop(0, NB)
    def _(i):
        r = pl.ds(pl.multiple_of(i * BQ, BQ), BQ)
        cosine, sine = angles(r)
        lane = lax.broadcasted_iota(jnp.int32, (BQ, 128), 1)
        for h in range(3):
            q = mixed_ref[r, h * 192 : h * 192 + 64]
            k = mixed_ref[r, h * 192 + 64 : h * 192 + 128]
            v = mixed_ref[r, h * 192 + 128 : h * 192 + 192]
            q = q.astype(F32) * cosine + dot(q, turn) * sine
            k = k.astype(F32) * cosine + dot(k, turn) * sine
            q = q.astype(BF) * 0.125
            qs[h, r] = q
            qt[h, i] = q.astype(F32).T.astype(BF)
            ks[h, r] = k.astype(BF)
            wide = jnp.concatenate([v.astype(F32), jnp.zeros((BQ, 64), F32)], axis=1)
            vs[h, r] = jnp.where((lane == 64) | (lane == 65), 1.0, wide).astype(BF)
            gs[h, r] = grad_ref[r, h * 64 : h * 64 + 64]

    @pl.loop(0, 3)
    def _(h):
        dkt[h] = jnp.zeros((64, 2048), F32)
        dvt[h] = jnp.zeros((64, 2048), F32)
        for i in range(NB):
            r = pl.ds(i * BQ, BQ)
            q = qs[h, r]
            start = table_ref[r, 80:81].astype(jnp.int32)
            top = None
            for b in range(i + 1):
                col = pl.ds(b * BQ, BQ)
                s = dot_nt(q, ks[h, col])
                cols = lax.broadcasted_iota(jnp.int32, (BQ, BQ), 1)
                keep = cols >= start - b * BQ
                if b == i:
                    keep &= cols <= lax.broadcasted_iota(jnp.int32, (BQ, BQ), 0)
                s = jnp.where(keep, s, -1e30)
                ss[:, col] = s
                m = jnp.max(s, axis=-1, keepdims=True)
                top = m if top is None else jnp.maximum(top, m)
            acc = None
            for b in range(i + 1):
                col = pl.ds(b * BQ, BQ)
                e = jnp.exp(ss[:, col] - top).astype(BF)
                es[:, col] = e
                o = dot(e, vs[h, col])
                acc = o if acc is None else acc + o
            inverse = 1.0 / acc[:, 64:65]
            o = acc[:, :64] * inverse
            os[h, r] = o.astype(BF)
            g = gs[h, r].astype(F32) * inverse
            delta = -jnp.sum(g * o, axis=-1, keepdims=True)
            high = delta.astype(BF).astype(F32)
            lane = lax.broadcasted_iota(jnp.int32, (BQ, 128), 1)
            wide = jnp.concatenate([g, jnp.zeros((BQ, 64), F32)], axis=1)
            wide = jnp.where(lane == 64, high, jnp.where(lane == 65, delta - high, wide)).astype(BF)
            gt = g.T.astype(BF)
            dq = None
            for b in range(i + 1):
                col = pl.ds(b * BQ, BQ)
                dp = dot_nt(wide, vs[h, col])
                e = es[:, col]
                ds = (e.astype(F32) * dp).astype(BF)
                part = dot(ds, ks[h, col])
                dq = part if dq is None else dq + part
                dkt[h, :, col] += dot(qt[h, i], ds)
                dvt[h, :, col] += dot(gt, e)
            dqs[h, r] = dq * 0.125

    @pl.loop(0, NB)
    def _(i):
        r = pl.ds(pl.multiple_of(i * BQ, BQ), BQ)
        cosine, sine = angles(r)

        def back(g):
            return g * cosine + dot_nt((g * sine).astype(BF), turn)

        parts = []
        for h in range(3):
            parts.append(back(dqs[h, r]))
            parts.append(back(dkt[h, :, r].T))
            parts.append(dvt[h, :, r].T)
        out_ref[r] = jnp.concatenate(parts, axis=1).astype(BF)
        ctx = jnp.concatenate([os[h, r].astype(F32) for h in range(3)], axis=1)
        ctx_ref[r] = ctx.astype(BF)
        ctxt_ref[:, r] = ctx.T.astype(BF)


def attention(mixed, table, grads):
    vm = pl.BlockSpec(memory_space=pltpu.VMEM)
    return pl.pallas_call(
        attention_kernel,
        out_shape=(
            jax.ShapeDtypeStruct((2048, 192), BF),
            jax.ShapeDtypeStruct((192, 2048), BF),
            jax.ShapeDtypeStruct((2048, 576), BF),
        ),
        in_specs=[vm] * 3,
        out_specs=[vm] * 3,
        scratch_shapes=[
            pltpu.VMEM((3, 2048, 64), BF),
            pltpu.VMEM((3, 2048, 64), BF),
            pltpu.VMEM((3, 2048, 128), BF),
            pltpu.VMEM((3, NB, 64, BQ), BF),
            pltpu.VMEM((BQ, 2048), BF),
            pltpu.VMEM((BQ, 2048), F32),
            pltpu.VMEM((3, 64, 2048), F32),
            pltpu.VMEM((3, 64, 2048), F32),
            pltpu.VMEM((3, 2048, 64), F32),
            pltpu.VMEM((3, 2048, 64), BF),
            pltpu.VMEM((3, 2048, 64), BF),
        ],
        compiler_params=pltpu.CompilerParams(vmem_limit_bytes=VMEM_LIMIT),
        cost_estimate=pl.CostEstimate(
            flops=30_000_000_000, bytes_accessed=10_000_000, transcendentals=8_000_000
        ),
        name="attention_both",
    )(mixed, table, grads)


def tail_kernel(
    ctx_h, ctxt_h, mg_h, act_h, actt_h, dg_h, unitt_h, w_h, vec_ref, ga_h, gb_h, gc_h, gd_h, rows_ref,
    out_ref, back_ref, fin_ref,
    ctx, ctxt, mg, act, actt, hl, unitt, w, g, buf, passed, got, grads, first_in, second_in, part, third_in, col,
    ld, sa, ra, sb, rb, s0, r0, s1, r1, s2, r2, s3, r3, s4, r4,
):
    x, z, y, c = places()
    is0 = c == 0
    me = lax.axis_index("shard")
    right, left = lax.rem(x + 1, 4), lax.rem(x + 3, 4)
    sibling = (x, me + 1 - 2 * c)

    def tok(k):
        return pl.ds(pl.multiple_of(lax.rem(x + 4 - k, 4) * 512, 512), 512)

    loads = []

    def load(src, dst):
        cp = pltpu.make_async_copy(src, dst, ld.at[len(loads)])
        cp.start()
        loads.append(cp)
        return cp

    l_ctx = load(ctx_h, ctx)
    l_w = load(w_h, w)
    l_act = load(act_h, act)
    l_g = [load(s, g.at[tok(k)]) for k, s in enumerate((ga_h, gb_h, gc_h, gd_h))]
    l_dg = load(dg_h, hl)
    l_mg = load(mg_h, mg)
    l_unitt = load(unitt_h, unitt)
    l_actt = load(actt_h, actt)
    l_ctxt = load(ctxt_h, ctxt)

    def first(k):
        return at(x, jnp.where(is0, lax.rem(z + k, 4), z), jnp.where(is0, y, lax.rem(y + k, 4)), c)

    def second(k):
        return at(x, jnp.where(is0, z, lax.rem(z + k, 4)), jnp.where(is0, lax.rem(y + k, 4), y), c)

    here1 = jnp.where(is0, z, y)
    here2 = jnp.where(is0, y, z)

    def rows(a, b, flip):
        blk = jnp.where(is0 != flip, a * 4 + b, b * 4 + a)
        return pl.ds(pl.multiple_of(blk * PAIR, 16), PAIR)

    barrier = pltpu.get_barrier_semaphore()
    peers = [first(k) for k in (1, 2, 3)] + [second(k) for k in (1, 2, 3)] + [sibling]
    peers += [(lax.rem(x + k, 4), me) for k in (1, 2, 3)]
    for peer in peers:
        pl.semaphore_signal(barrier, inc=1, device_id=peer, device_id_type=MESH)
    pl.semaphore_wait(barrier, len(peers))
    started = []

    def remote(src, dst, ss, rs, dev):
        cp = pltpu.make_async_remote_copy(
            src_ref=src, dst_ref=dst, send_sem=ss, recv_sem=rs, device_id=dev, device_id_type=MESH
        )
        return cp

    def send(*args):
        cp = remote(*args)
        cp.start()
        started.append(cp)

    def landed(dst, sem):
        remote(dst, dst, sem, sem, sibling).wait_recv()

    half = [pl.ds(0, 256), pl.ds(256, 256)]
    dev_x = [(right, me), (left, me)]

    def far_send(n):
        for d in range(2):
            send(buf.at[n, 2, half[d]], passed.at[n, d], sa.at[n, d], ra.at[n, d], dev_x[d])

    def near_send(n, d, h):
        send(buf.at[n, 3 - 2 * d, half[h]], got.at[n, d, half[h]], sb.at[n, d, h], rb.at[n, d, h], dev_x[d])

    def pass_on(n):
        for d in range(2):
            landed(passed.at[n, d], ra.at[n, d])
            k = 3 - 2 * d
            buf[n, k, half[d]] = (buf[n, k, half[d]].astype(F32) + passed[n, d].astype(F32)).astype(BF)
            near_send(n, d, d)

    def total(n, h):
        for d in range(2):
            landed(got.at[n, d, half[h]], rb.at[n, d, h])
        return buf[n, 0, half[h]].astype(F32) + got[n, 0, half[h]].astype(F32) + got[n, 1, half[h]].astype(F32)

    out_rows = pl.ds(pl.multiple_of(x * 192, 64), 192)

    def outputs_of(k):
        base = lax.rem(x + 4 - k, 4) * 512

        @pl.loop(0, 2)
        def _(i):
            r = pl.ds(pl.multiple_of(base + i * 256, 256), 256)
            o = dot(ctx[r], w[0, out_rows, 0:768]) + dot(act[r], w[1, :, 768:])
            buf[0, k, pl.ds(pl.multiple_of(i * 256, 256), 256)] = o.astype(BF)

    def pulls_of(k):
        base = lax.rem(x + 4 - k, 4) * 512

        @pl.loop(0, 2)
        def _(i):
            r = pl.ds(pl.multiple_of(base + i * 256, 256), 256)
            ag = dot_nt(g[r], w[1, :, 768:])
            low = (ag * hl[r].astype(F32)).astype(BF)
            hl[r] = low
            s = dot_nt(low, w[1, :, 0:768]) * vec_ref[2:3] + dot_nt(mg[r], w[0, :, 768:1344]) * vec_ref[0:1]
            buf[1, k, pl.ds(pl.multiple_of(i * 256, 256), 256)] = s.astype(BF)

    l_ctx.wait()
    l_w.wait()
    l_act.wait()
    for k in (2, 3, 1, 0):
        outputs_of(k)
        if k == 2:
            far_send(0)
        elif k == 3:
            near_send(0, 0, 1)
        elif k == 1:
            near_send(0, 1, 0)
    for cp in l_g:
        cp.wait()
    l_dg.wait()
    l_mg.wait()
    for k in (2, 3, 1, 0):
        pulls_of(k)
        if k == 2:
            far_send(1)
            pass_on(0)
        elif k == 3:
            near_send(1, 0, 1)
        elif k == 1:
            near_send(1, 1, 0)
    l_unitt.wait()
    l_actt.wait()
    l_ctxt.wait()
    ones = jnp.ones((16, 2048), BF)
    sum_mix = dot(ones, mg[...])[0:8]
    sum_up = dot(ones, hl[...])[0:8]
    sum_g = dot(ones, g[...])[0:8]
    gains = jnp.concatenate([vec_ref[...], sum_up, sum_g], axis=0)
    col[...] = jnp.concatenate([gains, jnp.zeros((104, 768), F32)], axis=0).T

    grads[0, :, 0:768] = jnp.zeros((768, 768), BF)
    grads[0, out_rows, 0:768] = dot(ctxt[...], g[...]).astype(BF)

    @pl.loop(0, 3)
    def _(i):
        r = pl.ds(pl.multiple_of(i * 256, 256), 256)
        cols = col[r]

        def over_tokens(a, b):
            return sum(dot(a[n, r], b[n * 512 : n * 512 + 512]) for n in range(4))

        u1 = over_tokens(unitt, mg)
        wm = w[0, r, 768:1344].astype(F32)
        gain1 = jnp.sum(wm * u1, axis=-1, keepdims=True)
        shift1 = jnp.sum(wm * sum_mix[0:1], axis=-1, keepdims=True)
        dmix = u1 * cols[:, 0:1] + cols[:, 1:2] * sum_mix[0:1]
        u2 = over_tokens(unitt, hl)
        wu = w[1, r, 0:768].astype(F32)
        gain2 = jnp.sum(wu * u2, axis=-1, keepdims=True)
        shift2 = jnp.sum(wu * sum_up[0:1], axis=-1, keepdims=True)
        grads[1, r, 0:768] = (u2 * cols[:, 2:3] + cols[:, 3:4] * sum_up[0:1]).astype(BF)
        grads[1, r, 768:] = over_tokens(actt, g).astype(BF)
        lane = lax.broadcasted_iota(jnp.int32, (256, 192), 1)
        small = jnp.zeros((256, 192), F32)
        for n, v in enumerate((gain1, shift1, gain2, shift2, cols[:, 16:17], cols[:, 8:9])):
            small = jnp.where(lane == n, v, small)
        grads[0, r, 768:1536] = jnp.concatenate([dmix, small], axis=1).astype(BF)

    mixcol = jnp.concatenate([sum_mix, jnp.zeros((120, 576), F32)], axis=0).T
    col[pl.ds(0, 576)] = mixcol
    lane = lax.broadcasted_iota(jnp.int32, (192, 192), 1)
    more = jnp.zeros((192, 192), F32)
    for n in range(3):
        more = jnp.where(lane == 6 + n, col[pl.ds(n, 192, stride=3), 0:1], more)
    old = grads[0, out_rows, 768:1536].astype(F32)
    grads[0, out_rows, 768:1536] = (
        old + jnp.concatenate([jnp.zeros((192, 576), F32), more], axis=1)
    ).astype(BF)

    order = (1, 3, 2, 0)
    for k in order:
        for b in range(4):
            r = rows(lax.rem(here2 + k, 4), b, True)
            send(grads.at[1 - c, r], first_in.at[r], s0.at[k, b], r0.at[k, b], sibling)
    pass_on(1)
    for k in order:
        place = lax.rem(here1 + k, 4)
        for b in range(4):
            r = rows(place, b, False)
            landed(first_in.at[r], r0.at[k, b])
            grads[c, r] = (grads[c, r].astype(F32) + first_in[r].astype(F32)).astype(BF)
            if k:
                send(grads.at[c, r], second_in.at[k - 1, b], s1.at[k - 1, b], r1.at[k - 1, b], first(k))
    for h in range(2):
        o = total(0, h) + rows_ref[half[h]].astype(F32) + vec_ref[4:5]
        out_ref[half[h]] = o.astype(BF)
    for j in order:
        b = lax.rem(here2 + j, 4)
        r = rows(here1, b, False)
        acc = grads[c, r].astype(F32)
        for k in (1, 3, 2):
            landed(second_in.at[k - 1, b], r1.at[k - 1, b])
            acc = acc + second_in[k - 1, b].astype(F32)
        part[j] = acc.astype(BF)
        if j:
            send(part.at[j], third_in.at[j - 1], s2.at[j - 1], r2.at[j - 1], second(j))
    acc = part[0].astype(F32)
    for j in (1, 3, 2):
        landed(third_in.at[j - 1], r2.at[j - 1])
        acc = acc + third_in[j - 1].astype(F32)
    fin_ref[c, x] = acc.astype(BF)
    for k in (1, 3, 2):
        slot = fin_ref.at[c, x]
        send(slot, slot, s3.at[k - 1], r3.at[k - 1], (lax.rem(x + k, 4), me))
    slot = fin_ref.at[c, x]
    send(slot, slot, s4.at[0], r4.at[0], sibling)
    for h in range(2):
        s = total(1, h)
        v = rows_ref[half[h]].astype(F32)
        v = v - jnp.mean(v, axis=-1, keepdims=True)
        inverse = lax.rsqrt(jnp.mean(v * v, axis=-1, keepdims=True) + 1e-05)
        unit = v * inverse
        s = s - jnp.mean(s, axis=-1, keepdims=True) - unit * jnp.mean(s * unit, axis=-1, keepdims=True)
        own = pl.ds(pl.multiple_of(x * 512 + h * 256, 256), 256)
        back_ref[half[h]] = (g[own].astype(F32) + inverse * s).astype(BF)
    for k in (1, 3, 2):
        slot = fin_ref.at[c, lax.rem(x + 4 - k, 4)]
        landed(slot, r3.at[k - 1])
        send(slot, slot, s4.at[k], r4.at[k], sibling)
    for k in range(4):
        landed(fin_ref.at[1 - c, lax.rem(x + 4 - k, 4)], r4.at[k])
    for cp in started:
        cp.wait_send()


def tail(ctx, ctxt, mg, act, actt, dg, unitt, w, vec, g, rows):
    vm = pl.BlockSpec(memory_space=pltpu.VMEM)
    hbm = pl.BlockSpec(memory_space=pl.ANY)
    dma = pltpu.SemaphoreType.DMA
    return pl.pallas_call(
        tail_kernel,
        out_shape=(
            jax.ShapeDtypeStruct((512, 768), BF),
            jax.ShapeDtypeStruct((512, 768), BF),
            jax.ShapeDtypeStruct((2, 4, PAIR, WIDE), BF),
        ),
        in_specs=[hbm] * 8 + [vm] + [hbm] * 4 + [vm],
        out_specs=[vm, vm, vm],
        scratch_shapes=[
            pltpu.VMEM((2048, 192), BF),
            pltpu.VMEM((192, 2048), BF),
            pltpu.VMEM((2048, 576), BF),
            pltpu.VMEM((2048, 768), BF),
            pltpu.VMEM((4, 768, 512), BF),
            pltpu.VMEM((2048, 768), BF),
            pltpu.VMEM((4, 768, 512), BF),
            pltpu.VMEM((2, 768, WIDE), BF),
            pltpu.VMEM((2048, 768), BF),
            pltpu.VMEM((2, 4, 512, 768), BF),
            pltpu.VMEM((2, 2, 256, 768), BF),
            pltpu.VMEM((2, 2, 512, 768), BF),
            pltpu.VMEM((2, 768, WIDE), BF),
            pltpu.VMEM((768, WIDE), BF),
            pltpu.VMEM((3, 4, PAIR, WIDE), BF),
            pltpu.VMEM((4, PAIR, WIDE), BF),
            pltpu.VMEM((3, PAIR, WIDE), BF),
            pltpu.VMEM((768, 128), F32),
            dma((12,)),
            dma((2, 2)), dma((2, 2)), dma((2, 2, 2)), dma((2, 2, 2)),
            dma((4, 4)), dma((4, 4)), dma((3, 4)), dma((3, 4)), dma((3,)), dma((3,)),
            dma((3,)), dma((3,)), dma((4,)), dma((4,)),
        ],
        compiler_params=pltpu.CompilerParams(
            collective_id=1, has_side_effects=True, vmem_limit_bytes=60 * 1024 * 1024
        ),
        name="tail_all",
    )(ctx, ctxt, mg, act, actt, dg, unitt, w, vec, *g, rows)


def shift_x(v, k):
    return lax.ppermute(v, "seq", [(i, (i + k) % NX) for i in range(NX)])


def swap_core(v):
    return lax.ppermute(v, "shard", [(i, i ^ 1) for i in range(32)])


def local(
    inputs, positions, first_gain, first_shift, second_gain, second_shift, mix_weight, mix_bias,
    out_weight, out_bias, up_weight, up_bias, down_weight, down_bias, cotangent,
):
    x, _, _, c = places()
    is0 = c == 0
    none = functools.partial(jnp.zeros, dtype=BF)
    vectors = (first_gain, first_shift, second_gain, second_shift, out_bias, down_bias, none((48,)))
    flat = jnp.concatenate(vectors + (mix_bias, up_bias, none((24,))))
    packed = jnp.concatenate([flat.reshape(2, 192), none((22, 192))], axis=0)
    half_a = jnp.concatenate(
        [
            out_weight,
            lax.dynamic_slice_in_dim(mix_weight, x * 576, 576, 1),
            packed,
        ],
        axis=1,
    )
    up_part = lax.dynamic_index_in_dim(up_weight.reshape(24, 32, 4, 24), x, 2, keepdims=False)
    half_b = jnp.concatenate(
        [up_part.reshape(24, 768), lax.dynamic_slice_in_dim(down_weight, x * 24, 24, 0)], axis=1
    )
    kept = jnp.where(is0, half_a, half_b)
    came = swap_core(jnp.where(is0, half_b, half_a))
    pair = jnp.where(is0, jnp.concatenate([kept, came], 0), jnp.concatenate([came, kept], 0))
    pos_own = jnp.concatenate([positions.reshape(4, 128)] * 2, axis=0)
    grad = cotangent[0]
    mixed, act, actt, slope, unitt, context_grad, w, vec, table = front(inputs[0], grad, pair, pos_own)
    late, table = lax.optimization_barrier((grad, table))
    grads = [grad] + [shift_x(late, k) for k in (1, 2, 3)]
    context, context_t, mix_grad = attention(mixed, table, context_grad)
    outputs, input_grad, shares = tail(
        context, context_t, mix_grad, act, actt, slope, unitt, w, vec, grads, inputs[0]
    )
    shares = lax.dynamic_slice_in_dim(shares, c * 24, 24, 2).astype(F32)
    half_a, half_b = shares[0], shares[1]
    got_out = jnp.sum(half_a[:, :, :768], axis=0)
    got_mix = half_a[:, :, 768:1344].transpose(1, 0, 2).reshape(24, 2304)
    got_small = jnp.sum(half_a[:, :, 1344:1353], axis=0)
    got_bias = half_a[0, :, 1348]
    got_up = half_b[:, :, :768].reshape(4, 24, 32, 24).transpose(1, 2, 0, 3).reshape(24, 3072)
    got_down = half_b[:, :, 768:].reshape(96, 768)
    return (
        outputs[None],
        input_grad[None],
        got_small[:, 0],
        got_small[:, 1],
        got_small[:, 2],
        got_small[:, 3],
        got_mix,
        got_small[:, 6:9].reshape(72),
        got_out,
        got_bias,
        got_up,
        half_a[:, :, 1349].reshape(96),
        got_down,
        got_bias,
    )


def solution(mesh):
    vec, mat, tok = P("shard"), P("shard", None), P("shard", "seq", None)
    return jax.shard_map(
        local,
        mesh=mesh,
        in_specs=(tok, P("shard", "seq"), vec, vec, vec, vec, mat, vec, mat, vec, mat, vec, mat, vec, tok),
        out_specs=(tok, tok, vec, vec, vec, vec, mat, vec, mat, vec, mat, vec, mat, vec),
        check_vma=False,
    )
```

profile of v0, /device:TPU:1, one launch (start us, length us, event | category | flops | bytes accessed | tf_op | source)
XLA Modules:
  0.0 211.8 jit_solution(1069100287267195246)
XLA Ops:
  0.6 0.0 copy-start
  0.7 0.0 copy-start.1
  0.7 5.5 %concatenate.21 = bf16[384]{0:T(512)(128)(2,1)S(1)} concatenate(bf16[24]{0:T(256)(128)(2,1)} %param.17, bf16[24]{0:T(256)(128)(2,1)} %param.18, bf16[24]{0:T(256)(128)(2,1)} %param.19, bf16[24]{0:T(256)(128)(2,1)} %param.20, bf16[24]{0:T(256)(128)(2,1)} %param.24, bf16[24]{0:T(256)(128)(2,1)} %param.28, bf16[48]{0:T(256)(128)(2,1)S(1)} %broadcast_in_dim.10, bf16[72]{0:T(256)(128)(2,1)} %param.22, ...), dimensions={0} | concatenate | bytes 1536 | tf_op jit(solution)/shard_map/concatenate | solution.py:745
  6.2 0.1 reshape.56
  6.3 2.1 reshape.57
  8.4 1.3 dynamic-slice_reduce_fusion
  9.7 0.3 reshape.58
  10.0 0.9 constant_dynamic-slice_fusion.1
  10.9 0.0 copy-done
  10.9 0.9 concatenate.23
  11.8 2.0 collective-permute-start
  13.8 1.4 pad_add_fusion.pos_ref
  15.1 0.0 collective-permute-done
  15.1 0.7 maximum_select_fusion.pair_ref
  15.8 48.3 %front_all.1 = (bf16[2048,576]{1,0:T(8,128)(2,1)}, bf16[2048,768]{1,0:T(8,128)(2,1)}, bf16[4,768,512]{2,1,0:T(8,128)(2,1)}, bf16[2048,768]{1,0:T(8,128)(2,1)}, b...) custom-call(bf16[512,768]{1,0:T(8,128)(2,1)} %bitcast.14, ...), custom_call_target="tpu_custom_call" | custom-call | tf_op jit(solution)/shard_map/front_all/pallas_call | solution.py:278
  64.2 0.0 copy-done.1
  64.2 1.6 collective-permute-start.3
  65.7 0.6 collective-permute-start.2
  66.4 0.1 collective-permute-start.1
  66.4 54.7 %attention_both.1 = (bf16[2048,192]{1,0:T(8,128)(2,1)}, bf16[192,2048]{1,0:T(8,128)(2,1)}, bf16[2048,576]{1,0:T(8,128)(2,1)}) custom-call(bf16[2048,576]{1,0:T(8,128)(2,1)} %get-tuple-element.31.mixed_ref, f32[2048,128]{1,0:T(8,128)} %get-tuple-element.33.table_ref, bf16[2048,192]{1,0:T(8,128)(2,1)} %get-tuple-element.34.grad_ref), custom_call_target="tpu_custom_call" | custom-call | flops 30000001024 | bytes 10000000 | tf_op jit(solution)/shard_map/attention_both/pallas_call | solution.py:413
  121.1 0.0 collective-permute-done.3.gd_h
  121.1 0.0 collective-permute-done.2.gc_h
  121.2 0.0 collective-permute-done.1.gb_h
  121.2 0.0 copy-start.4
  121.2 0.9 copy-done.2
  122.0 0.3 copy-done.3
  122.3 0.2 copy-done.4
  122.5 74.5 %tail_all.1 = (bf16[512,768]{1,0:T(8,128)(2,1)}, bf16[512,768]{1,0:T(8,128)(2,1)}, bf16[2,4,48,1536]{3,2,1,0:T(8,128)(2,1)}) custom-call(bf16[2048,192]{1,0:T(8,128)(2,1)} %get-tuple-element.35.ctx_h, bf16[192,2048]{1,0:T(8,128)(2,1)} %get-tuple-element.36.ctxt_h, bf16[2048,576]{1,0:T(8,128)(2,1)} %get-tuple-element.37.mg_h, ...), custom_call_target="tpu_custom_call" | custom-call | tf_op jit(solution)/shard_map/tail_all/pallas_call | solution.py:689
  197.0 1.2 dynamic-slice_convert_fusion
  198.2 0.1 slice_bitcast_fusion
  198.3 0.2 slice_reduce_fusion.3
  198.5 0.2 slice_reduce_fusion.1
  198.7 0.1 slice_reduce_fusion.2
  198.8 0.7 slice_reduce_fusion.4
  199.5 0.1 slice.63
  199.6 0.6 reshape_squeeze.3
  200.2 0.6 reshape.61
  200.8 1.4 fusion
  202.2 0.1 copy.31
  202.3 0.9 reshape.60
  203.2 1.1 reshape.62
  204.3 1.2 copy.32
  205.6 0.0 copy-start.5
  205.6 2.6 %reshape.63 = f32[24,3072]{1,0:T(8,128)} reshape(f32[24,32,4,24]{3,2,1,0:T(4,128)S(1)} %copy.32) | data formatting | bytes 589824 | tf_op jit(solution)/shard_map/reshape | solution.py:777
  208.1 0.5 copy.36
  208.6 2.1 copy.37
  210.7 0.0 copy-done.5
  210.7 0.9 copy.38
  (10 shorter events, 0.1 us)
Async XLA Ops:
  0.6 10.2 %copy-start = (bf16[96,768]{1,0:T(8,128)(2,1)S(1)}, bf16[96,768]{1,0:T(8,128)(2,1)}, u32[]{:S(2)}) copy-start(bf16[96,768]{1,0:T(8,128)(2,1)} %param.27) | copy-start | bytes 442372
  0.7 63.5 %copy-start.1 = (bf16[1,512,768]{2,1,0:T(8,128)(2,1)S(1)}, bf16[1,512,768]{2,1,0:T(8,128)(2,1)}, u32[]{:S(2)}) copy-start(bf16[1,512,768]{2,1,0:T(8,128)(2,1)} %param.29) | copy-start | bytes 2359300
  11.8 3.4 %collective-permute-start = (bf16[24,1536]{1,0:T(8,128)(2,1)S(1)}, bf16[24,1536]{1,0:T(8,128)(2,1)S(1)}, u32[]{:S(2)}, u32[]{:S(2)}) collective-permute-start(bf16[24,1536]{1,0:T(8,128)(2,1)S(1)} %get-tuple-element.57), channel_id=1, source_target_pairs={{0,1},{1,0},{2,3},{3,2},{4,5},{5,4},{6,7},{7,6},{8,9},{9,8},{10,11... | collective-permute-start | bytes 221192 | tf_op jit(solution)/shard_map/ppermute | solution.py:734
  64.2 57.0 %collective-permute-start.3 = (bf16[512,768]{1,0:T(8,128)(2,1)S(1)}, bf16[512,768]{1,0:T(8,128)(2,1)S(1)}, u32[]{:S(2)}, u32[]{:S(2)}) collective-permute-start(bf16[512,768]{1,0:T(8,128)(2,1)S(1)} %bitcast.18), channel_id=1, source_target_pairs={{0,96},{32,0},{64,32},{96,64},{1,97},{33,1},{65,33},{97,65},{2,98}... | collective-permute-start | bytes 2359304 | tf_op jit(solution)/shard_map/ppermute | solution.py:730
  65.7 55.4 %collective-permute-start.2 = (bf16[512,768]{1,0:T(8,128)(2,1)S(1)}, bf16[512,768]{1,0:T(8,128)(2,1)S(1)}, u32[]{:S(2)}, u32[]{:S(2)}) collective-permute-start(bf16[512,768]{1,0:T(8,128)(2,1)S(1)} %bitcast.19), channel_id=1, source_target_pairs={{0,64},{32,96},{64,0},{96,32},{1,65},{33,97},{65,1},{97,33},{2,66}... | collective-permute-start | bytes 2359304 | tf_op jit(solution)/shard_map/ppermute | solution.py:730
  66.4 54.8 %collective-permute-start.1 = (bf16[512,768]{1,0:T(8,128)(2,1)S(1)}, bf16[512,768]{1,0:T(8,128)(2,1)S(1)}, u32[]{:S(2)}, u32[]{:S(2)}) collective-permute-start(bf16[512,768]{1,0:T(8,128)(2,1)S(1)} %bitcast.20), channel_id=1, source_target_pairs={{0,32},{32,64},{64,96},{96,0},{1,33},{33,65},{65,97},{97,1},{2,34}... | collective-permute-start | bytes 2359304 | tf_op jit(solution)/shard_map/ppermute | solution.py:730
  121.1 0.9 copy-start.2
  121.2 1.2 copy-start.3
  121.2 1.4 copy-start.4
  198.5 9.6 %copy-start.6 = (f32[24]{0:T(128)}, f32[24]{0:T(128)S(1)}, u32[]{:S(2)}) copy-start(f32[24]{0:T(128)S(1)} %slice_reduce_fusion.3) | copy-start | bytes 292
  205.6 5.1 %copy-start.5 = (bf16[512,768]{1,0:T(8,128)(2,1)S(1)}, bf16[512,768]{1,0:T(8,128)(2,1)}, u32[]{:S(2)}) copy-start(bf16[512,768]{1,0:T(8,128)(2,1)} %get-tuple-element.46) | copy-start | bytes 2359300
where the time goes:
time: 215 us; the launch traced here: 212 us
  Pallas kernels  178 us (83%)
  local copies, waits for them, and re-layouts  24.2 us (11%)
  other arithmetic  4.75 us (2%)
  starting transfers between devices  4.25 us (2%)
    pallas_call x1, Pallas kernels, tail(): pl.pallas_call(tail_kernel, out_shape=(jax.ShapeDtypeStruct((512, 768), B...  74.5 us
    pallas_call x1, Pallas kernels, attention(): pl.pallas_call(attention_kernel, out_shape=(jax.ShapeDtypeStruct((2048, 1...  54.7 us
    pallas_call x1, Pallas kernels, front(): pl.pallas_call(front_kernel, out_shape=tuple((jax.ShapeDtypeStruct(s, t)...  48.3 us
    concatenate x1, local copies, waits for them, and re-layouts, local(): flat = jnp.concatenate(vectors + (mix_bias, up_bias, none((24,))))  5.51 us
    unnamed x17, local copies, waits for them, and re-layouts  4.84 us
  transfers between devices with their start and end apart: 4, of which 0 were waited for; matrix products, arithmetic and copies ran while one was open for 1% of the time, Pallas kernels for 26%

commit v1 on v0

--- a/solution.py
+++ b/solution.py
@@ -1,5 +1,3 @@
-import functools
-
 import jax
 import jax.numpy as jnp
 from jax import lax
@@ -60,7 +58,7 @@
 def front_kernel(
     rows_ref, grad_ref, pair_ref, pos_ref,
     mixed_o, act_o, actt_o, slope_o, unitt_o, cg_o, w_o, vec_o, table_o,
-    rows_all, w, pos_all, grad, mixed, act, actt, slope, unitt, cg, cgs, vec, table,
+    rows_all, units, w, pos_all, grad, mixed, act, actt, slope, unitt, cg, cgs, vec, table,
     s1, r1, s2, r2, s3, r3, sx, rx, sf, rf, sp, rp, sc, rc, loc, wr,
 ):
     x, z, y, c = places()
@@ -141,6 +139,25 @@
     for cp in local_copies:
         cp.wait()
 
+    writes = []
+
+    def write(src, dst):
+        cp = pltpu.make_async_copy(src, dst, wr.at[len(writes)])
+        cp.start()
+        writes.append(cp)
+
+    def norm(who):
+        @pl.loop(0, 2)
+        def _(i):
+            r = pl.ds(pl.multiple_of(who * 512 + i * 256, 256), 256)
+            v = rows_all[r].astype(F32)
+            v = v - jnp.mean(v, axis=-1, keepdims=True)
+            unit = v * lax.rsqrt(jnp.mean(v * v, axis=-1, keepdims=True) + 1e-05)
+            units[r] = unit
+            unitt[who, :, pl.ds(pl.multiple_of(i * 256, 256), 256)] = unit.astype(BF).T
+
+        write(unitt.at[who], unitt_o.at[who])
+
     for k in order:
         b = held(k, 0)
         landed(rows_of(mine, b), r1.at[k - 1])
@@ -148,6 +165,7 @@
             send(rows_of(mine, b), rows_of(mine, b), s2.at[k, j - 1], r2.at[k, j - 1], second(j))
         send(rows_of(mine, b), rows_of(mine, b), s3.at[k, 0], r3.at[k, 0], sibling)
 
+    norm(x)
     for k in order:
         src = lax.rem(x + 4 - k, 4)
         landed(pos_all.at[pl.ds(pl.multiple_of(src * 8, 8), 8)], rp.at[k - 1])
@@ -174,6 +192,11 @@
             b = held(k, j)
             landed(rows_of(mine, b), r2.at[k, j - 1])
             send(rows_of(mine, b), rows_of(mine, b), s3.at[k, j], r3.at[k, j], sibling)
+    for i in range(2):
+        landed(quarter(left, 2 + i), rx.at[0, 2 + i])
+        landed(quarter(right, i), rx.at[1, i])
+    norm(left)
+    norm(right)
     for a in range(4):
         for b in range(4):
             da, db = (4 - a) % 4, (4 - b) % 4
@@ -210,13 +233,6 @@
     up_b = spread(pick[1], 768, 72 + 24 * x, 24, 0)
     vec[...] = jnp.concatenate([g1, b1, g2, b2, out_b + down_b, up_b, g1, g1], axis=0)
 
-    writes = []
-
-    def write(src, dst):
-        cp = pltpu.make_async_copy(src, dst, wr.at[len(writes)])
-        cp.start()
-        writes.append(cp)
-
     write(w, w_o)
     write(vec, vec_o)
     write(table, table_o)
@@ -225,11 +241,8 @@
         @pl.loop(0, 2)
         def _(i):
             r = pl.ds(pl.multiple_of(who * 512 + i * 256, 256), 256)
-            v = rows_all[r].astype(F32)
-            v = v - jnp.mean(v, axis=-1, keepdims=True)
-            unit = v * lax.rsqrt(jnp.mean(v * v, axis=-1, keepdims=True) + 1e-05)
             cols = pl.ds(pl.multiple_of(i * 256, 256), 256)
-            unitt[who, :, cols] = unit.astype(BF).T
+            unit = units[r]
             one = (unit * vec[0:1] + vec[1:2]).astype(BF)
             mixed[r] = (dot(one, w[0, :, 768:1344]) + mix_b).astype(BF)
             two = (unit * vec[2:3] + vec[3:4]).astype(BF)
@@ -245,18 +258,14 @@
         write(act.at[t], act_o.at[t])
         write(slope.at[t], slope_o.at[t])
         write(actt.at[who], actt_o.at[who])
-        write(unitt.at[who], unitt_o.at[who])
 
     compute(x)
-    for i in range(2):
-        landed(quarter(left, 2 + i), rx.at[0, 2 + i])
     compute(left)
-    for i in range(2):
-        landed(quarter(right, i), rx.at[1, i])
     compute(right)
     for i in range(2):
         landed(quarter(far, i), rf.at[0, i])
         landed(quarter(far, 3 - i), rf.at[1, i])
+    norm(far)
     compute(far)
     for k in (1, 3, 2):
         t = pl.ds(pl.multiple_of(lax.rem(x + 4 - k, 4) * 512, 512), 512)
@@ -282,6 +291,7 @@
         out_specs=[hbm] * 9,
         scratch_shapes=[
             pltpu.VMEM((2048, 768), BF),
+            pltpu.VMEM((2048, 768), F32),
             pltpu.VMEM((2, 768, WIDE), BF),
             pltpu.VMEM((32, 128), jnp.int32),
             pltpu.VMEM((512, 768), BF),
@@ -305,27 +315,32 @@
     )(rows, grad, pair, pos)
 
 
-BQ = 512
+BQ = 256
 NB = 2048 // BQ
 
 
 def attention_kernel(
     mixed_ref, table_ref, grad_ref, ctx_ref, ctxt_ref, out_ref,
-    qs, ks, vs, qt, es, ss, dkt, dvt, dqs, os, gs,
+    qs, ks, vs, qt, ea, eb, sa, sb, dkt, dvt, dqs, os, gs,
 ):
     row, lane = iota((64, 64), 0), iota((64, 64), 1)
     turn = jnp.where((lane == row + 8) & (row < 8), 1.0, jnp.where((row == lane + 8) & (lane < 8), -1.0, 0.0))
     turn = turn.astype(BF)
+    scores, expd = (sa, sb), (ea, eb)
 
     def angles(r):
         t = table_ref[r]
-        return t[:, 0:64], jnp.where(iota((BQ, 64), 1) < ROT, t[:, 64:128], 0.0)
-
-    @pl.loop(0, NB)
+        return t[:, 0:64], jnp.where(iota((512, 64), 1) < ROT, t[:, 64:128], 0.0)
+
+    def with_lanes(v, first, second):
+        lane = iota((v.shape[0], 128), 1)
+        wide = jnp.concatenate([v, jnp.zeros((v.shape[0], 64), F32)], axis=1)
+        return jnp.where(lane == 64, first, jnp.where(lane == 65, second, wide)).astype(BF)
+
+    @pl.loop(0, 4)
     def _(i):
-        r = pl.ds(pl.multiple_of(i * BQ, BQ), BQ)
+        r = pl.ds(pl.multiple_of(i * 512, 512), 512)
         cosine, sine = angles(r)
-        lane = lax.broadcasted_iota(jnp.int32, (BQ, 128), 1)
         for h in range(3):
             q = mixed_ref[r, h * 192 : h * 192 + 64]
             k = mixed_ref[r, h * 192 + 64 : h * 192 + 128]
@@ -334,73 +349,81 @@
             k = k.astype(F32) * cosine + dot(k, turn) * sine
             q = q.astype(BF) * 0.125
             qs[h, r] = q
-            qt[h, i] = q.astype(F32).T.astype(BF)
+            qt[h, :, r] = q.astype(F32).T.astype(BF)
             ks[h, r] = k.astype(BF)
-            wide = jnp.concatenate([v.astype(F32), jnp.zeros((BQ, 64), F32)], axis=1)
-            vs[h, r] = jnp.where((lane == 64) | (lane == 65), 1.0, wide).astype(BF)
+            vs[h, r] = with_lanes(v.astype(F32), 1.0, 1.0)
             gs[h, r] = grad_ref[r, h * 64 : h * 64 + 64]
 
     @pl.loop(0, 3)
     def _(h):
         dkt[h] = jnp.zeros((64, 2048), F32)
         dvt[h] = jnp.zeros((64, 2048), F32)
-        for i in range(NB):
-            r = pl.ds(i * BQ, BQ)
-            q = qs[h, r]
+        top, wide, grad_t = {}, {}, {}
+
+        def score(i):
+            r, n = pl.ds(i * BQ, BQ), (i + 1) * BQ
+            s = dot_nt(qs[h, r], ks[h, 0:n])
             start = table_ref[r, 80:81].astype(jnp.int32)
-            top = None
-            for b in range(i + 1):
-                col = pl.ds(b * BQ, BQ)
-                s = dot_nt(q, ks[h, col])
-                cols = lax.broadcasted_iota(jnp.int32, (BQ, BQ), 1)
-                keep = cols >= start - b * BQ
-                if b == i:
-                    keep &= cols <= lax.broadcasted_iota(jnp.int32, (BQ, BQ), 0)
-                s = jnp.where(keep, s, -1e30)
-                ss[:, col] = s
-                m = jnp.max(s, axis=-1, keepdims=True)
-                top = m if top is None else jnp.maximum(top, m)
-            acc = None
-            for b in range(i + 1):
-                col = pl.ds(b * BQ, BQ)
-                e = jnp.exp(ss[:, col] - top).astype(BF)
-                es[:, col] = e
-                o = dot(e, vs[h, col])
-                acc = o if acc is None else acc + o
+            middle = 512 <= i * BQ < 1536
+            parts = []
+            for a in range(0, n, BQ):
+                part = s[:, a : a + BQ]
+                cols = iota((BQ, BQ), 1)
+                keep = None if middle and a >= 512 else cols >= start - a
+                if a + BQ == n:
+                    causal = cols <= iota((BQ, BQ), 0)
+                    keep = causal if keep is None else keep & causal
+                parts.append(part if keep is None else jnp.where(keep, part, -1e30))
+            s = jnp.concatenate(parts, axis=1)
+            scores[i % 2][:, 0:n] = s
+            m = s[:, 0:128]
+            for t in range(128, n, 128):
+                m = jnp.maximum(m, s[:, t : t + 128])
+            top[i] = jnp.max(m, axis=-1, keepdims=True)
+
+        def probs(i):
+            r, n = pl.ds(i * BQ, BQ), (i + 1) * BQ
+            e = jnp.exp(scores[i % 2][:, 0:n] - top[i]).astype(BF)
+            expd[i % 2][:, 0:n] = e
+            acc = dot(e, vs[h, 0:n])
             inverse = 1.0 / acc[:, 64:65]
             o = acc[:, :64] * inverse
             os[h, r] = o.astype(BF)
             g = gs[h, r].astype(F32) * inverse
             delta = -jnp.sum(g * o, axis=-1, keepdims=True)
             high = delta.astype(BF).astype(F32)
-            lane = lax.broadcasted_iota(jnp.int32, (BQ, 128), 1)
-            wide = jnp.concatenate([g, jnp.zeros((BQ, 64), F32)], axis=1)
-            wide = jnp.where(lane == 64, high, jnp.where(lane == 65, delta - high, wide)).astype(BF)
-            gt = g.T.astype(BF)
-            dq = None
-            for b in range(i + 1):
-                col = pl.ds(b * BQ, BQ)
-                dp = dot_nt(wide, vs[h, col])
-                e = es[:, col]
-                ds = (e.astype(F32) * dp).astype(BF)
-                part = dot(ds, ks[h, col])
-                dq = part if dq is None else dq + part
-                dkt[h, :, col] += dot(qt[h, i], ds)
-                dvt[h, :, col] += dot(gt, e)
-            dqs[h, r] = dq * 0.125
-
-    @pl.loop(0, NB)
+            wide[i] = with_lanes(g, high, delta - high)
+            grad_t[i] = g.T.astype(BF)
+
+        def back(i):
+            r, n = pl.ds(i * BQ, BQ), (i + 1) * BQ
+            dp = dot_nt(wide[i], vs[h, 0:n])
+            e = expd[i % 2][:, 0:n]
+            ds = e * dp.astype(BF)
+            dqs[h, r] = dot(ds, ks[h, 0:n]) * 0.125
+            dkt[h, :, 0:n] += dot(qt[h, :, r], ds)
+            dvt[h, :, 0:n] += dot(grad_t[i], e)
+
+        for step in range(NB + 2):
+            if step >= 2:
+                back(step - 2)
+            if 1 <= step <= NB:
+                probs(step - 1)
+            if step < NB:
+                score(step)
+
+    @pl.loop(0, 4)
     def _(i):
-        r = pl.ds(pl.multiple_of(i * BQ, BQ), BQ)
+        r = pl.ds(pl.multiple_of(i * 512, 512), 512)
         cosine, sine = angles(r)
 
-        def back(g):
+        def unturn(g):
             return g * cosine + dot_nt((g * sine).astype(BF), turn)
 
         parts = []
         for h in range(3):
-            parts.append(back(dqs[h, r]))
-            parts.append(back(dkt[h, :, r].T))
+            parts.append(unturn(dqs[h, r]))
+            parts.append(unturn(dkt[h, :, r].T))
             parts.append(dvt[h, :, r].T)
         out_ref[r] = jnp.concatenate(parts, axis=1).astype(BF)
         ctx = jnp.concatenate([os[h, r].astype(F32) for h in range(3)], axis=1)
@@ -423,8 +446,10 @@
             pltpu.VMEM((3, 2048, 64), BF),
             pltpu.VMEM((3, 2048, 64), BF),
             pltpu.VMEM((3, 2048, 128), BF),
-            pltpu.VMEM((3, NB, 64, BQ), BF),
+            pltpu.VMEM((3, 64, 2048), BF),
             pltpu.VMEM((BQ, 2048), BF),
+            pltpu.VMEM((BQ, 2048), BF),
+            pltpu.VMEM((BQ, 2048), F32),
             pltpu.VMEM((BQ, 2048), F32),
             pltpu.VMEM((3, 64, 2048), F32),
             pltpu.VMEM((3, 64, 2048), F32),
@@ -442,8 +467,8 @@
 
 def tail_kernel(
     ctx_h, ctxt_h, mg_h, act_h, actt_h, dg_h, unitt_h, w_h, vec_ref, ga_h, gb_h, gc_h, gd_h, rows_ref,
-    out_ref, back_ref, fin_ref,
-    ctx, ctxt, mg, act, actt, hl, unitt, w, g, buf, passed, got, grads, first_in, second_in, part, third_in, col,
+    out_ref, back_ref, wout_ref, wmix_ref, wup_ref, wdown_ref, small_ref,
+    ctx, ctxt, mg, act, actt, hl, unitt, w, g, buf, passed, got, grads, first_in, second_in, part, third_in, fin_ref, col,
     ld, sa, ra, sb, rb, s0, r0, s1, r1, s2, r2, s3, r3, s4, r4,
 ):
     x, z, y, c = places()
@@ -572,11 +597,11 @@
         pulls_of(k)
         if k == 2:
             far_send(1)
-            pass_on(0)
         elif k == 3:
             near_send(1, 0, 1)
         elif k == 1:
             near_send(1, 1, 0)
+    pass_on(0)
     l_unitt.wait()
     l_actt.wait()
     l_ctxt.wait()
@@ -631,7 +656,6 @@
         for b in range(4):
             r = rows(lax.rem(here2 + k, 4), b, True)
             send(grads.at[1 - c, r], first_in.at[r], s0.at[k, b], r0.at[k, b], sibling)
-    pass_on(1)
     for k in order:
         place = lax.rem(here1 + k, 4)
         for b in range(4):
@@ -640,9 +664,13 @@
             grads[c, r] = (grads[c, r].astype(F32) + first_in[r].astype(F32)).astype(BF)
             if k:
                 send(grads.at[c, r], second_in.at[k - 1, b], s1.at[k - 1, b], r1.at[k - 1, b], first(k))
-    for h in range(2):
-        o = total(0, h) + rows_ref[half[h]].astype(F32) + vec_ref[4:5]
-        out_ref[half[h]] = o.astype(BF)
+    pass_on(1)
+    lane = iota((1, WIDE), 1)
+    group = lax.rem(lax.div(lane, 24), 4)
+    source = lax.div(lane, 96) * 24 + lax.rem(lane, 24)
+    for d in range(4):
+        hot = iota((384, WIDE), 0) == jnp.where(group == d, source, -1)
+        w[d // 2, (d % 2) * 384 : (d % 2) * 384 + 384] = hot.astype(F32).astype(BF)
     for j in order:
         b = lax.rem(here2 + j, 4)
         r = rows(here1, b, False)
@@ -653,6 +681,9 @@
         part[j] = acc.astype(BF)
         if j:
             send(part.at[j], third_in.at[j - 1], s2.at[j - 1], r2.at[j - 1], second(j))
+    for h in range(2):
+        o = total(0, h) + rows_ref[half[h]].astype(F32) + vec_ref[4:5]
+        out_ref[half[h]] = o.astype(BF)
     acc = part[0].astype(F32)
     for j in (1, 3, 2):
         landed(third_in.at[j - 1], r2.at[j - 1])
@@ -678,6 +709,27 @@
         send(slot, slot, s4.at[k], r4.at[k], sibling)
     for k in range(4):
         landed(fin_ref.at[1 - c, lax.rem(x + 4 - k, 4)], r4.at[k])
+
+    def mine(role, d, a, b):
+        v = fin_ref[role, d, :, a:b].astype(F32)
+        return jnp.where(is0, v[0:24], v[24:48])
+
+    wout_ref[...] = sum(mine(0, d, 0, 768) for d in range(4))
+    tails = [mine(0, d, 768, WIDE) for d in range(4)]
+    wmix_ref[...] = jnp.concatenate([t[:, 0:576] for t in tails], axis=1)
+    lane = iota((24, 128), 1)
+    small = sum(t[:, 576:704] for t in tails)
+    for d in range(4):
+        small = jnp.where(lane == 16 + d, tails[d][:, 581:582], small)
+    small_ref[...] = jnp.where(lane == 4, tails[0][:, 576:704], small)
+    ups = [mine(1, d, 0, 768).astype(BF) for d in range(4)]
+    for n in range(2):
+        wup_ref[:, n * WIDE : n * WIDE + WIDE] = sum(
+            dot(ups[d][:, n * 384 : n * 384 + 384], w[d // 2, (d % 2) * 384 : (d % 2) * 384 + 384])
+            for d in range(4)
+        )
+    for d in range(4):
+        wdown_ref[d * 24 : d * 24 + 24] = mine(1, d, 768, WIDE)
     for cp in started:
         cp.wait_send()
 
@@ -691,10 +743,14 @@
         out_shape=(
             jax.ShapeDtypeStruct((512, 768), BF),
             jax.ShapeDtypeStruct((512, 768), BF),
-            jax.ShapeDtypeStruct((2, 4, PAIR, WIDE), BF),
+            jax.ShapeDtypeStruct((24, 768), F32),
+            jax.ShapeDtypeStruct((24, 2304), F32),
+            jax.ShapeDtypeStruct((24, 3072), F32),
+            jax.ShapeDtypeStruct((96, 768), F32),
+            jax.ShapeDtypeStruct((24, 128), F32),
         ),
         in_specs=[hbm] * 8 + [vm] + [hbm] * 4 + [vm],
-        out_specs=[vm, vm, vm],
+        out_specs=[vm] * 7,
         scratch_shapes=[
             pltpu.VMEM((2048, 192), BF),
             pltpu.VMEM((192, 2048), BF),
@@ -713,6 +769,7 @@
             pltpu.VMEM((3, 4, PAIR, WIDE), BF),
             pltpu.VMEM((4, PAIR, WIDE), BF),
             pltpu.VMEM((3, PAIR, WIDE), BF),
+            pltpu.VMEM((2, 4, PAIR, WIDE), BF),
             pltpu.VMEM((768, 128), F32),
             dma((12,)),
             dma((2, 2)), dma((2, 2)), dma((2, 2, 2)), dma((2, 2, 2)),
@@ -740,10 +797,13 @@
 ):
     x, _, _, c = places()
     is0 = c == 0
-    none = functools.partial(jnp.zeros, dtype=BF)
-    vectors = (first_gain, first_shift, second_gain, second_shift, out_bias, down_bias, none((48,)))
-    flat = jnp.concatenate(vectors + (mix_bias, up_bias, none((24,))))
-    packed = jnp.concatenate([flat.reshape(2, 192), none((22, 192))], axis=0)
+    flat = jnp.zeros((384,), BF)
+    for place, v in (
+        (0, first_gain), (24, first_shift), (48, second_gain), (72, second_shift), (96, out_bias),
+        (120, down_bias), (192, mix_bias), (264, up_bias),
+    ):
+        flat = flat + jnp.pad(v, (place, 384 - place - v.shape[0]))
+    packed = jnp.pad(flat.reshape(2, 192), ((0, 22), (0, 0)))
     half_a = jnp.concatenate(
         [
             out_weight,
@@ -765,32 +825,24 @@
     late, table = lax.optimization_barrier((grad, table))
     grads = [grad] + [shift_x(late, k) for k in (1, 2, 3)]
     context, context_t, mix_grad = attention(mixed, table, context_grad)
-    outputs, input_grad, shares = tail(
+    outputs, input_grad, g_out, g_mix, g_up, g_down, small = tail(
         context, context_t, mix_grad, act, actt, slope, unitt, w, vec, grads, inputs[0]
     )
-    shares = lax.dynamic_slice_in_dim(shares, c * 24, 24, 2).astype(F32)
-    half_a, half_b = shares[0], shares[1]
-    got_out = jnp.sum(half_a[:, :, :768], axis=0)
-    got_mix = half_a[:, :, 768:1344].transpose(1, 0, 2).reshape(24, 2304)
-    got_small = jnp.sum(half_a[:, :, 1344:1353], axis=0)
-    got_bias = half_a[0, :, 1348]
-    got_up = half_b[:, :, :768].reshape(4, 24, 32, 24).transpose(1, 2, 0, 3).reshape(24, 3072)
-    got_down = half_b[:, :, 768:].reshape(96, 768)
     return (
         outputs[None],
         input_grad[None],
-        got_small[:, 0],
-        got_small[:, 1],
-        got_small[:, 2],
-        got_small[:, 3],
-        got_mix,
-        got_small[:, 6:9].reshape(72),
-        got_out,
-        got_bias,
-        got_up,
-        half_a[:, :, 1349].reshape(96),
-        got_down,
-        got_bias,
+        small[:, 0],
+        small[:, 1],
+        small[:, 2],
+        small[:, 3],
+        g_mix,
+        small[:, 6:9].reshape(72),
+        g_out,
+        small[:, 4],
+        g_up,
+        small[:, 16:20].T.reshape(96),
+        g_down,
+        small[:, 4],
     )
 
 

time: 215 us -> 191 us (0.89)
  Pallas kernels: 178 us -> 160 us
  local copies, waits for them, and re-layouts: 24.2 us -> 18.8 us
    pallas_call x1, Pallas kernels: 54.7 us -> 39.9 us  [attention(): pl.pallas_call(attention_kernel, out_shape=(jax.ShapeDtypeStruct((2048, 1...]
    concatenate x2 -> x0, local copies, waits for them, and re-layouts: 5.52 us -> none  [the longest x1 5.51 us: local(): flat = jnp.concatenate(vectors + (mix_bias, up_bias, none((24,))))]
    reshape x5 -> x3, local copies, waits for them, and re-layouts: 5.26 us -> 1.29 us  [the longest x1 0.61 us: local(): small[:, 6:9].reshape(72)]
    unnamed x17 -> x27, local copies, waits for them, and re-layouts: 4.84 us -> 8.78 us
    pallas_call x1, Pallas kernels: 74.5 us -> 72.2 us  [tail(): pl.pallas_call(tail_kernel, out_shape=(jax.ShapeDtypeStruct((512, 768), B...]
  transfers between devices with their start and end apart: 4 -> 4, of which waited for: 0 -> 0; matrix products, arithmetic and copies ran while one was open for 1% -> 1% of each run, Pallas kernels for 26% -> 21%
where the time goes in v1:
time: 191 us; the launch traced here: 188 us
  Pallas kernels  160 us (84%)
  local copies, waits for them, and re-layouts  18.8 us (10%)
  starting transfers between devices  4.74 us (2%)
  other arithmetic  2.99 us (2%)
    pallas_call x1, Pallas kernels, tail(): pl.pallas_call(tail_kernel, out_shape=(jax.ShapeDtypeStruct((512, 768), B...  72.2 us
    pallas_call x1, Pallas kernels, front(): pl.pallas_call(front_kernel, out_shape=tuple((jax.ShapeDtypeStruct(s, t)...  48 us
    pallas_call x1, Pallas kernels, attention(): pl.pallas_call(attention_kernel, out_shape=(jax.ShapeDtypeStruct((2048, 1...  39.9 us
    unnamed x27, local copies, waits for them, and re-layouts  8.78 us
  transfers between devices with their start and end apart: 4, of which 0 were waited for; matrix products, arithmetic and copies ran while one was open for 1% of the time, Pallas kernels for 21%

profile of v1, /device:TPU:1, one launch (start us, length us, event | category | flops | bytes accessed | tf_op | source)
XLA Modules:
  0.0 187.7 jit_solution(12304964553296039570)
XLA Ops:
  0.6 0.0 copy-start
  0.7 0.0 copy-start.1
  0.7 0.9 pad_add_fusion.1
  1.6 0.1 reshape.47
  1.7 2.1 %reshape.48 = bf16[24,32,4,24]{3,2,1,0:T(4,128)(2,1)S(1)} reshape(bf16[24,3072]{1,0:T(8,128)(2,1)} %param.25) | data formatting | bytes 294912 | tf_op jit(solution)/shard_map/reshape | solution.py:815
  3.8 1.3 dynamic-slice_reduce_fusion
  5.1 0.3 reshape.49
  5.4 0.9 constant_dynamic-slice_fusion.1
  6.2 0.0 copy-done
  6.3 0.9 concatenate.15
  7.2 2.0 %collective-permute-start = (bf16[24,1536]{1,0:T(8,128)(2,1)S(1)}, bf16[24,1536]{1,0:T(8,128)(2,1)S(1)}, u32[]{:S(2)}, u32[]{:S(2)}) collective-permute-start(bf16[24,1536]{1,0:T(8,128)(2,1)S(1)} %get-tuple-element.62), channel_id=1, source_target_pairs={{0,1},{1,0},{2,3},{3,2},{4,5},{5,4},{6,7},{7,6},{8,9},{9,8},{10,11... | collective-permute-start | bytes 221192 | tf_op jit(solution)/shard_map/ppermute | solution.py:791
  9.2 1.4 pad_add_fusion.pos_ref
  10.5 0.0 collective-permute-done
  10.5 0.7 maximum_select_fusion.pair_ref
  11.2 48.0 %front_all.1 = (bf16[2048,576]{1,0:T(8,128)(2,1)}, bf16[2048,768]{1,0:T(8,128)(2,1)}, bf16[4,768,512]{2,1,0:T(8,128)(2,1)}, bf16[2048,768]{1,0:T(8,128)(2,1)}, b...) custom-call(bf16[512,768]{1,0:T(8,128)(2,1)} %bitcast.7, ...), custom_call_target="tpu_custom_call" | custom-call | tf_op jit(solution)/shard_map/front_all/pallas_call | solution.py:287
  59.2 0.0 copy-done.1
  59.3 1.9 %collective-permute-start.3 = (bf16[512,768]{1,0:T(8,128)(2,1)S(1)}, bf16[512,768]{1,0:T(8,128)(2,1)S(1)}, u32[]{:S(2)}, u32[]{:S(2)}) collective-permute-start(bf16[512,768]{1,0:T(8,128)(2,1)S(1)} %bitcast.11), channel_id=1, source_target_pairs={{0,96},{32,0},{64,32},{96,64},{1,97},{33,1},{65,33},{97,65},{2,98}... | collective-permute-start | bytes 2359304 | tf_op jit(solution)/shard_map/ppermute | solution.py:787
  61.1 0.6 collective-permute-start.2
  61.8 0.2 collective-permute-start.1
  62.0 39.9 %attention_both.1 = (bf16[2048,192]{1,0:T(8,128)(2,1)}, bf16[192,2048]{1,0:T(8,128)(2,1)}, bf16[2048,576]{1,0:T(8,128)(2,1)}) custom-call(bf16[2048,576]{1,0:T(8,128)(2,1)} %get-tuple-element.35.mixed_ref, f32[2048,128]{1,0:T(8,128)} %get-tuple-element.37.table_ref, bf16[2048,192]{1,0:T(8,128)(2,1)} %get-tuple-element.38.grad_ref), custom_call_target="tpu_custom_call" | custom-call | flops 30000001024 | bytes 10000000 | tf_op jit(solution)/shard_map/attention_both/pallas_call | solution.py:436
  101.9 0.0 collective-permute-done.3.gd_h
  101.9 0.0 collective-permute-done.2.gc_h
  101.9 0.0 copy-start.3
  101.9 0.0 collective-permute-done.1.gb_h
  101.9 0.0 copy-start.4
  101.9 0.8 copy-done.2
  102.8 0.3 copy-done.3
  103.0 0.2 copy-done.4
  103.3 72.2 %tail_all.1 = (bf16[512,768]{1,0:T(8,128)(2,1)}, bf16[512,768]{1,0:T(8,128)(2,1)}, f32[24,768]{1,0:T(8,128)}, f32[24,2304]{1,0:T(8,128)}, f32[24,3072]{1,0:T(8,1...) custom-call(bf16[2048,192]{1,0:T(8,128)(2,1)} %get-tuple-element.39.ctx_h, bf16[192,2048]{1,0:T(8,128)(2,1)} %get-tuple-element.40.ctxt_h, ...), custom_call_target="tpu_custom_call" | custom-call | tf_op jit(solution)/shard_map/tail_all/pallas_call | solution.py:741
  175.5 0.0 copy-start.7
  175.5 0.0 copy-start.8
  175.5 0.0 copy-start.6
  175.5 0.0 copy-start.5
  175.5 1.7 slice_reduce_fusion
  177.2 0.8 slice.26
  178.0 0.8 slice_bitcast_fusion
  178.8 0.6 reshape.51
  179.4 0.1 copy.31
  179.5 0.6 reshape.52
  180.1 0.5 copy.39
  180.6 2.1 %copy.40 = bf16[1,512,768]{2,1,0:T(8,128)(2,1)} copy(bf16[1,512,768]{2,1,0:T(8,128)(2,1)} %bitcast.15) | data formatting | bytes 1572864
  182.6 2.1 %copy.41 = bf16[1,512,768]{2,1,0:T(8,128)(2,1)} copy(bf16[1,512,768]{2,1,0:T(8,128)(2,1)} %bitcast.14) | data formatting | bytes 1572864
  184.7 0.0 copy-done.7
  184.7 0.7 copy.42
  185.4 0.0 copy-done.8
  185.4 0.6 copy.43
  186.0 0.7 copy.44
  186.7 0.7 copy.45
  (8 shorter events, 0.1 us)
Async XLA Ops:
  0.6 5.6 %copy-start = (bf16[96,768]{1,0:T(8,128)(2,1)S(1)}, bf16[96,768]{1,0:T(8,128)(2,1)}, u32[]{:S(2)}) copy-start(bf16[96,768]{1,0:T(8,128)(2,1)} %param.27) | copy-start | bytes 442372
  0.7 58.6 %copy-start.1 = (bf16[1,512,768]{2,1,0:T(8,128)(2,1)S(1)}, bf16[1,512,768]{2,1,0:T(8,128)(2,1)}, u32[]{:S(2)}) copy-start(bf16[1,512,768]{2,1,0:T(8,128)(2,1)} %param.29) | copy-start | bytes 2359300
  7.2 3.4 %collective-permute-start = (bf16[24,1536]{1,0:T(8,128)(2,1)S(1)}, bf16[24,1536]{1,0:T(8,128)(2,1)S(1)}, u32[]{:S(2)}, u32[]{:S(2)}) collective-permute-start(bf16[24,1536]{1,0:T(8,128)(2,1)S(1)} %get-tuple-element.62), channel_id=1, source_target_pairs={{0,1},{1,0},{2,3},{3,2},{4,5},{5,4},{6,7},{7,6},{8,9},{9,8},{10,11... | collective-permute-start | bytes 221192 | tf_op jit(solution)/shard_map/ppermute | solution.py:791
  59.3 42.6 %collective-permute-start.3 = (bf16[512,768]{1,0:T(8,128)(2,1)S(1)}, bf16[512,768]{1,0:T(8,128)(2,1)S(1)}, u32[]{:S(2)}, u32[]{:S(2)}) collective-permute-start(bf16[512,768]{1,0:T(8,128)(2,1)S(1)} %bitcast.11), channel_id=1, source_target_pairs={{0,96},{32,0},{64,32},{96,64},{1,97},{33,1},{65,33},{97,65},{2,98}... | collective-permute-start | bytes 2359304 | tf_op jit(solution)/shard_map/ppermute | solution.py:787
  61.1 40.7 %collective-permute-start.2 = (bf16[512,768]{1,0:T(8,128)(2,1)S(1)}, bf16[512,768]{1,0:T(8,128)(2,1)S(1)}, u32[]{:S(2)}, u32[]{:S(2)}) collective-permute-start(bf16[512,768]{1,0:T(8,128)(2,1)S(1)} %bitcast.12), channel_id=1, source_target_pairs={{0,64},{32,96},{64,0},{96,32},{1,65},{33,97},{65,1},{97,33},{2,66}... | collective-permute-start | bytes 2359304 | tf_op jit(solution)/shard_map/ppermute | solution.py:787
  61.8 40.1 %collective-permute-start.1 = (bf16[512,768]{1,0:T(8,128)(2,1)S(1)}, bf16[512,768]{1,0:T(8,128)(2,1)S(1)}, u32[]{:S(2)}, u32[]{:S(2)}) collective-permute-start(bf16[512,768]{1,0:T(8,128)(2,1)S(1)} %bitcast.13), channel_id=1, source_target_pairs={{0,32},{32,64},{64,96},{96,0},{1,33},{33,65},{65,97},{97,1},{2,34}... | collective-permute-start | bytes 2359304 | tf_op jit(solution)/shard_map/ppermute | solution.py:787
  101.9 0.9 copy-start.2
  101.9 1.1 copy-start.3
  101.9 1.4 copy-start.4
  175.5 9.2 %copy-start.7 = (f32[24,2304]{1,0:T(8,128)S(1)}, f32[24,2304]{1,0:T(8,128)}, u32[]{:S(2)}) copy-start(f32[24,2304]{1,0:T(8,128)} %get-tuple-element.111) | copy-start | bytes 663556
  175.5 9.9 %copy-start.8 = (f32[24,768]{1,0:T(8,128)S(1)}, f32[24,768]{1,0:T(8,128)}, u32[]{:S(2)}) copy-start(f32[24,768]{1,0:T(8,128)} %get-tuple-element.113) | copy-start | bytes 221188
  175.5 10.5 %copy-start.6 = (f32[24,3072]{1,0:T(8,128)S(1)}, f32[24,3072]{1,0:T(8,128)}, u32[]{:S(2)}) copy-start(f32[24,3072]{1,0:T(8,128)} %get-tuple-element.115) | copy-start | bytes 884740
  175.5 11.2 %copy-start.5 = (f32[96,768]{1,0:T(8,128)S(1)}, f32[96,768]{1,0:T(8,128)}, u32[]{:S(2)}) copy-start(f32[96,768]{1,0:T(8,128)} %get-tuple-element.117) | copy-start | bytes 884740
  177.2 10.2 %copy-start.9 = (f32[24]{0:T(128)}, f32[24]{0:T(128)S(1)}, u32[]{:S(2)}) copy-start(f32[24]{0:T(128)S(1)} %get-tuple-element.114) | copy-start | bytes 292
